TPU v7x, 512 devices: a whole 4x4x16 slice. The times are simulated.
512 devices in a mesh: row: 32 (over z, y_hi), col: 16 (over y_lo, x, core).
Axes of the slice: x: 4, y: 4 (y_hi: 2, y_lo: 2; y = y_hi * 2 + y_lo), z: 16, core: 2. Of those that a mesh axis runs over, the one named last changes fastest.
Arguments:
- features: float32 [65536, 128], P(('row', 'col')), may hold values from -6 to 6
- weight: float32 [128, 128], replicated, may hold values from -0.5 to 0.5
- grad_out: float32 [65536, 128], P(('row', 'col')), may hold values from -6 to 6
- adj_tiles: bfloat16 [32, 16, 16, 128, 128], P('row', 'col'), may hold values from 0 to 0.2795085
- tile_rows: int32 [32, 16, 16], P('row', 'col'), may hold values from 0 to 15
- tile_cols: int32 [32, 16, 16], P('row', 'col'), may hold values from 0 to 31
- tile_count: int32 [32, 16], P('row', 'col'), may hold values from 1 to 16, as said below
Outputs:
- activated: float32 [65536, 128], P(('row', 'col'))
- grad_in: float32 [65536, 128], P(('row', 'col'))
Inputs may be any that keep to these rules, and one draw needn't show every extreme that they name: `tile_count`: some device block has exactly 16 live slots.
All inputs are finite; a program needn't handle non-finite values.
Results may differ from a plain program's by a relative error of at most 0.005.
Values sent between devices are 32-bit elements; how exact they have to be, the bound alone decides.
A program may use at most 64 MiB of HBM per device.

v0:
```python
import jax
import jax.numpy as jnp
from jax import lax
from jax.sharding import PartitionSpec as P


def combine(tiles_in, take_index, put_index, live_mask, source, slot_count, transposed):
    chosen = jnp.take(source, take_index, axis=0)
    pattern = "tab,taf->tbf" if transposed else "tab,tbf->taf"
    products = jnp.einsum(
        pattern, tiles_in.astype(jnp.float32), chosen, precision=lax.Precision.HIGHEST
    )
    products = products * live_mask[:, None, None]
    one_hot = (put_index[:, None] == jnp.arange(slot_count, dtype=jnp.int32)[None, :]).astype(
        jnp.float32
    )
    return jnp.einsum("ts,taf->saf", one_hot, products, precision=lax.Precision.HIGHEST)


def aggregate(tiles_in, take_index, put_index, live_mask, source, slot_count, transposed):
    return combine(tiles_in, take_index, put_index, live_mask, source, slot_count, transposed)


def body(features, weight, grad_out, adj_tiles, tile_rows, tile_cols, tile_count):
    tiles_here = adj_tiles[0, 0]
    rows_here = tile_rows[0, 0]
    cols_here = tile_cols[0, 0]
    count_here = tile_count[0, 0]
    nodes_here, width = features.shape
    tile_size = tiles_here.shape[1]
    row_count = lax.axis_size("row")
    col_count = lax.axis_size("col")
    live_mask = (jnp.arange(tiles_here.shape[0], dtype=jnp.int32) < count_here).astype(jnp.float32)
    column_block = lax.all_gather(features, "row", axis=0, tiled=True)
    column_block = column_block.reshape(row_count * nodes_here // tile_size, tile_size, width)
    partial_value = aggregate(
        tiles_here,
        cols_here,
        rows_here,
        live_mask,
        column_block,
        col_count * nodes_here // tile_size,
        False,
    )
    partial_value = partial_value.reshape(col_count * nodes_here, width)
    summed = lax.psum(partial_value, "col")
    aggregated = lax.dynamic_slice_in_dim(summed, lax.axis_index("col") * nodes_here, nodes_here, 0)
    pre = jnp.dot(
        aggregated, weight, precision=lax.Precision.HIGHEST, preferred_element_type=jnp.float32
    )
    activated = jnp.maximum(pre, 0.0)
    masked = jnp.where(pre > 0.0, grad_out, 0.0)
    backed = lax.dot_general(
        masked,
        weight,
        (((1,), (1,)), ((), ())),
        precision=lax.Precision.HIGHEST,
        preferred_element_type=jnp.float32,
    )
    row_block = lax.all_gather(backed, "col", axis=0, tiled=True)
    row_block = row_block.reshape(col_count * nodes_here // tile_size, tile_size, width)
    partial_back = aggregate(
        tiles_here,
        rows_here,
        cols_here,
        live_mask,
        row_block,
        row_count * nodes_here // tile_size,
        True,
    )
    partial_back = partial_back.reshape(row_count * nodes_here, width)
    summed_back = lax.psum(partial_back, "row")
    grad_in = lax.dynamic_slice_in_dim(
        summed_back, lax.axis_index("row") * nodes_here, nodes_here, 0
    )
    return (activated, grad_in)


def solution(mesh):
    return jax.shard_map(
        body,
        mesh=mesh,
        in_specs=(
            P(("row", "col"), None),
            P(),
            P(("row", "col"), None),
            P("row", "col", None, None, None),
            P("row", "col", None),
            P("row", "col", None),
            P("row", "col"),
        ),
        out_specs=(P(("row", "col"), None), P(("row", "col"), None)),
        check_vma=False,
    )
```

profile of v0, /device:TPU:2, one launch (start us, length us, event | category | flops | bytes accessed | tf_op | source)
XLA Modules:
  0.0 675.4 jit_solution(13385177103233060824)
XLA Ops:
  7.2 0.0 all-gather.3.cloned.1.call-start
  7.2 0.7 all-gather.3.cloned.1.call-update
  7.9 0.0 all-reduce.3.cloned.1.call-start
  8.6 0.7 fusion.30
  9.3 0.7 compare_and_fusion.1
  9.9 155.8 %all-gather.3.cloned.1.call-done = f32[4096,128]{1,0:T(8,128)} async-done(((f32[128,128]{1,0:T(8,128)}), f32[4096,128]{1,0:T(8,128)}) %all-gather.3.cloned.1.call-update) | async-done | bytes 2097168 | tf_op jit(solution)/shard_map/all_gather | solution.py:34
  165.8 2.2 gather_fusion
  168.0 1.1 fusion.8
  169.1 0.5 copy.11
  169.6 0.7 fusion.2
  170.4 1.3 copy.9
  171.7 0.0 all-gather.5.cloned.1.call-start
  171.8 126.5 %all-reduce.3.cloned.1.call-done = f32[2048,128]{1,0:T(8,128)} async-done(((f32[2048,128]{1,0:T(8,128)}), f32[2048,128]{1,0:T(8,128)}) %all-reduce.3.cloned.1.call-update) | async-done | bytes 1048592 | tf_op jit(solution)/shard_map/psum | solution.py:46
  298.3 1.7 broadcast_maximum_fusion
  300.0 0.9 fusion.18
  300.9 0.0 all-reduce.5.cloned.1.call-start
  301.0 43.8 %all-gather.5.cloned.1.call-done = f32[2048,128]{1,0:T(8,128)} async-done(((f32[128,128]{1,0:T(8,128)}), f32[2048,128]{1,0:T(8,128)}) %all-gather.5.cloned.1.call-update) | async-done | bytes 1048592 | tf_op jit(solution)/shard_map/all_gather | solution.py:60
  344.8 1.8 gather_fusion.1
  346.6 1.1 fusion.5
  347.7 0.5 copy.12
  348.3 1.1 fusion
  349.4 2.5 copy.10
  351.9 315.4 %all-reduce.5.cloned.1.call-done = f32[4096,128]{1,0:T(8,128)} async-done(((f32[4096,128]{1,0:T(8,128)}), f32[4096,128]{1,0:T(8,128)}) %all-reduce.5.cloned.1.call-update) | async-done | bytes 2097168 | tf_op jit(solution)/shard_map/psum | solution.py:72
  667.4 1.5 constant_dynamic-slice_fusion
  (18 shorter events, 0.1 us)
Async XLA Ops:
  7.2 160.8 %copy-start = (bf16[1,1,16,128,128]{4,3,2,1,0:T(8,128)(2,1)S(1)}, bf16[1,1,16,128,128]{4,3,2,1,0:T(8,128)(2,1)}, u32[]{:S(2)}) copy-start(bf16[1,1,16,128,128]{4,3,2,1,0:T(8,128)(2,1)} %param.10) | copy-start | bytes 1572868
  7.2 158.6 %all-gather.3.cloned.1.call-start = ((), (), s32[]{:S(2)}) async-start(), calls=%async_computation | async-start | bytes 2162688 | tf_op jit(solution)/shard_map/all_gather | solution.py:34
  7.9 290.4 %all-reduce.3.cloned.1.call-start = ((), (), s32[]{:S(2)}) async-start(), calls=%async_computation.1 | async-start | bytes 2097152 | tf_op jit(solution)/shard_map/psum | solution.py:46
  168.0 1.6 copy-start.4
  170.4 128.0 %copy-start.1 = (f32[128,128]{1,0:T(8,128)S(1)}, f32[128,128]{1,0:T(8,128)}, u32[]{:S(2)}) copy-start(f32[128,128]{1,0:T(8,128)} %param.8) | copy-start | bytes 196612
  170.4 129.6 %copy-start.2 = (f32[128,128]{1,0:T(8,128)S(1)}, f32[128,128]{1,0:T(8,128)}, u32[]{:S(2)}) copy-start(f32[128,128]{1,0:T(8,128)} %param.9) | copy-start | bytes 196612
  171.7 173.0 %all-gather.5.cloned.1.call-start = ((), (), s32[]{:S(2)}) async-start(), calls=%async_computation.2 | async-start | bytes 1114112 | tf_op jit(solution)/shard_map/all_gather | solution.py:60
  300.9 366.5 %all-reduce.5.cloned.1.call-start = ((), (), s32[]{:S(2)}) async-start(), calls=%async_computation.3 | async-start | bytes 4194304 | tf_op jit(solution)/shard_map/psum | solution.py:72
  346.6 1.6 copy-start.3
Sparse Core Ops, SparseCore 0:
  11.1 154.6 all-gather.2
  171.9 126.4 all-reduce.2
  301.3 43.4 all-gather.4
  352.0 315.2 all-reduce.4
where the time goes:
time: 676 us; the launch traced here: 675 us
  waiting for transfers between devices  642 us (95%)
  between operations  14.6 us (2%)
  local copies, waits for them, and re-layouts  10.4 us (2%)
    psum x1, waiting for transfers between devices, body(): summed_back = lax.psum(partial_back, 'row')  315 us
    all_gather x1, waiting for transfers between devices, body(): column_block = lax.all_gather(features, 'row', axis=0, tiled=True)  156 us
    psum x1, waiting for transfers between devices, body(): summed = lax.psum(partial_value, 'col')  127 us
    all_gather x1, waiting for transfers between devices, body(): row_block = lax.all_gather(backed, 'col', axis=0, tiled=True)  43.8 us
  transfers between devices with their start and end apart: 4, of which 4 were waited for; matrix products, arithmetic and copies ran while one was open for 0% of the time, Pallas kernels for 0%

commit v1 on v0

v1 whole, which is shorter than its diff:
```python
import functools

import jax
import jax.numpy as jnp
from jax import lax
from jax.experimental import pallas as pl
from jax.experimental.pallas import tpu as pltpu
from jax.sharding import PartitionSpec as P

F32 = jnp.float32
BF16 = jnp.bfloat16
MESH = pl.DeviceIdType.MESH
B = 128
SLOTS = 16
NZ = 16
CHIPS = ((1, 2), (0, 2), (1, 1), (1, 3), (0, 1), (0, 3), (1, 0), (0, 0))


def split(value, parts):
    out = []
    for _ in range(parts - 1):
        head = value.astype(BF16)
        out.append(head)
        value = value - head.astype(F32)
    out.append(value.astype(BF16))
    return out


def tile_product(tile, value, parts, transposed):
    dims = (((0,), (0,)), ((), ())) if transposed else (((1,), (0,)), ((), ()))
    total = None
    for part in reversed(split(value, parts)):
        term = lax.dot_general(tile, part, dims, preferred_element_type=F32)
        total = term if total is None else total + term
    return total


def kernel(
    feat, weight, grad_out, tiles_hbm, rows, cols, count,
    act, grad_in,
    fbuf, tiles, acc, stage, sib, outb, rin, rowbuf, snd, rsin, total1, hx,
    prev_r, prev_c, last_r, last_c,
    tile_sem, px_s, px_r, ag_s, ag_r, sb_s, sb_r, rc_s, rc_r, cg_s, cg_r, cs_s, cs_r, rs_s, rs_r, hx_s, hx_r,
):
    me_row = lax.axis_index("row")
    me_col = lax.axis_index("col")
    z, h = me_row // 2, lax.rem(me_row, 2)
    core = lax.rem(me_col, 2)
    chip = me_col // 2
    y, x = chip // 4, lax.rem(chip, 4)

    def row_id(zz, q):
        return lax.rem(zz + 2 * NZ, NZ) * 2 + (h if q == 0 else 1 - h)

    def chip_to(k):
        dy, dx = CHIPS[k]
        return (lax.rem(y + dy, 2)) * 4 + lax.rem(x + dx, 4)

    def chip_from(k):
        dy, dx = CHIPS[k]
        return (lax.rem(y + dy, 2)) * 4 + lax.rem(x + 4 - dx, 4)

    sends = []

    def send(src, dst, s_sem, r_sem, dev):
        copy = pltpu.make_async_remote_copy(
            src_ref=src, dst_ref=dst, send_sem=s_sem, recv_sem=r_sem,
            device_id=dev, device_id_type=MESH,
        )
        copy.start()
        sends.append(copy)
        return copy

    ring = ((row_id(z + 1, 0), me_col), (row_id(z - 1, 0), me_col))
    partner = (row_id(z, 1), me_col)
    sibling = (me_row, chip * 2 + 1 - core)
    peers = [(me_row, chip_to(k) * 2 + core) for k in range(7)]

    tile_copy = pltpu.make_async_copy(tiles_hbm, tiles, tile_sem)
    tile_copy.start()

    barrier = pltpu.get_barrier_semaphore()
    everyone = list(ring) + [partner, sibling] + peers
    for dev in everyone:
        pl.semaphore_signal(barrier, inc=1, device_id=dev, device_id_type=MESH)
    pl.semaphore_wait(barrier, len(everyone))

    ag = {}
    for d in range(2):
        ag[d, 0, 0] = send(feat, fbuf.at[me_row], ag_s.at[d, 0, 0], ag_r.at[d, 0, 0], ring[d])
    px = send(feat, fbuf.at[me_row], px_s, px_r, partner)
    fbuf[me_row] = feat[...]

    live = count[0]
    key_r = [jnp.where(t < live, rows[t], -1 - t) for t in range(SLOTS)]
    key_c = [jnp.where(t < live, cols[t], -1 - t) for t in range(SLOTS)]
    for t in range(SLOTS):
        pr, pc = jnp.int32(SLOTS), jnp.int32(SLOTS)
        for u in range(t):
            pr = jnp.where(key_r[u] == key_r[t], u, pr)
            pc = jnp.where(key_c[u] == key_c[t], u, pc)
        prev_r[t] = pr
        prev_c[t] = pc
    for r in range(16):
        last = jnp.int32(SLOTS)
        for t in range(SLOTS):
            last = jnp.where(key_r[t] == r, t, last)
        last_r[r] = last
    for r in range(32):
        last = jnp.int32(SLOTS)
        for t in range(SLOTS):
            last = jnp.where(key_c[t] == r, t, last)
        last_c[r] = last
    acc[SLOTS] = jnp.zeros((B, B), F32)

    for s in range(8):
        for q in range(2):
            for d in range(2):
                if (s == 0 and q == 0) or (s == 7 and q != d):
                    continue
                if s == 0 and d == 0:
                    px.wait_recv()
                if s > 0:
                    ag[d, s - 1, q].wait_recv()
                block = row_id(z - s if d == 0 else z + s, q)
                ag[d, s, q] = send(
                    fbuf.at[block], fbuf.at[block], ag_s.at[d, s, q], ag_r.at[d, s, q], ring[d]
                )
    ag[0, 6, 1].wait_recv()
    ag[1, 6, 0].wait_recv()
    ag[0, 7, 0].wait_recv()
    ag[1, 7, 1].wait_recv()

    tile_copy.wait()
    for t in range(SLOTS):
        acc[t] = tile_product(tiles[t], fbuf[cols[t]], 3, False) + acc[prev_r[t]]

    sb, rc = [], []
    for k in range(8):
        stage[k] = acc[last_r[chip_to(k) * 2 + 1 - core]]
        sb.append(send(stage.at[k], sib.at[k], sb_s.at[k], sb_r.at[k], sibling))
    for k in range(8):
        mine = acc[last_r[chip_to(k) * 2 + core]]
        sb[k].wait_recv()
        outb[k] = mine + sib[k]
        if k < 7:
            rc.append(send(outb.at[k], rin.at[k], rc_s.at[k], rc_r.at[k], peers[k]))
    aggregated = outb[7]
    for k in reversed(range(7)):
        rc[k].wait_recv()
        aggregated = aggregated + rin[k]

    pre = jnp.dot(
        aggregated, weight[...], precision=lax.Precision.HIGHEST, preferred_element_type=F32
    )
    masked = jnp.where(pre > 0.0, grad_out[...], 0.0)
    rowbuf[me_col] = lax.dot_general(
        masked, weight[...], (((1,), (1,)), ((), ())),
        precision=lax.Precision.HIGHEST, preferred_element_type=F32,
    )

    cg, cs = [], []
    own = rowbuf.at[me_col]
    for k in range(7):
        cg.append(send(own, own, cg_s.at[k], cg_r.at[k], peers[k]))
    cs.append(send(own, own, cs_s.at[7], cs_r.at[7], sibling))
    act[...] = jnp.maximum(pre, 0.0)
    for k in reversed(range(7)):
        cg[k].wait_recv()
        block = rowbuf.at[chip_from(k) * 2 + core]
        cs.append(send(block, block, cs_s.at[k], cs_r.at[k], sibling))
    for copy in cs:
        copy.wait_recv()

    for t in range(SLOTS):
        acc[t] = tile_product(tiles[t], rowbuf[rows[t]], 2, True) + acc[prev_c[t]]

    rs = {}
    for s in range(8):
        for q in (1, 0):
            for d in range(2):
                if s == 0 and q != d:
                    continue
                block = row_id(z + 8 - s if d == 0 else z - 8 + s, q)
                mine = acc[last_c[block]]
                if (d, s - 1, q) in rs:
                    rs[d, s - 1, q].wait_recv()
                    mine = mine + rsin[d, s - 1, q]
                snd[d, s, q] = mine
                rs[d, s, q] = send(
                    snd.at[d, s, q], rsin.at[d, s, q], rs_s.at[d, s, q], rs_r.at[d, s, q], ring[d]
                )
    theirs = acc[last_c[row_id(z, 1)]]
    rs[0, 7, 1].wait_recv()
    rs[1, 7, 1].wait_recv()
    total1[...] = theirs + rsin[0, 7, 1] + rsin[1, 7, 1]
    across = send(total1, hx, hx_s, hx_r, partner)
    mine = acc[last_c[row_id(z, 0)]]
    rs[0, 7, 0].wait_recv()
    rs[1, 7, 0].wait_recv()
    mine = mine + rsin[0, 7, 0] + rsin[1, 7, 0]
    across.wait_recv()
    grad_in[...] = mine + hx[...]

    for copy in sends:
        copy.wait_send()


def body(features, weight, grad_out, adj_tiles, tile_rows, tile_cols, tile_count):
    vmem = pl.BlockSpec(memory_space=pltpu.VMEM)
    smem = pl.BlockSpec(memory_space=pltpu.SMEM)
    dma = pltpu.SemaphoreType.DMA
    return pl.pallas_call(
        kernel,
        out_shape=[jax.ShapeDtypeStruct((B, B), F32)] * 2,
        in_specs=[vmem, vmem, vmem, pl.BlockSpec(memory_space=pl.ANY), smem, smem, smem],
        out_specs=[vmem, vmem],
        scratch_shapes=[
            pltpu.VMEM((32, B, B), F32),
            pltpu.VMEM((SLOTS, B, B), BF16),
            pltpu.VMEM((SLOTS + 1, B, B), F32),
            pltpu.VMEM((8, B, B), F32),
            pltpu.VMEM((8, B, B), F32),
            pltpu.VMEM((8, B, B), F32),
            pltpu.VMEM((7, B, B), F32),
            pltpu.VMEM((16, B, B), F32),
            pltpu.VMEM((2, 8, 2, B, B), F32),
            pltpu.VMEM((2, 8, 2, B, B), F32),
            pltpu.VMEM((B, B), F32),
            pltpu.VMEM((B, B), F32),
            pltpu.SMEM((SLOTS,), jnp.int32),
            pltpu.SMEM((SLOTS,), jnp.int32),
            pltpu.SMEM((16,), jnp.int32),
            pltpu.SMEM((32,), jnp.int32),
            dma(()), dma(()), dma(()),
            dma((2, 8, 2)), dma((2, 8, 2)),
            dma((8,)), dma((8,)),
            dma((7,)), dma((7,)),
            dma((7,)), dma((7,)),
            dma((8,)), dma((8,)),
            dma((2, 8, 2)), dma((2, 8, 2)),
            dma(()), dma(()),
        ],
        compiler_params=pltpu.CompilerParams(
            collective_id=0, has_side_effects=True, vmem_limit_bytes=40 * 1024 * 1024
        ),
        name="graph_layer",
    )(
        features, weight, grad_out,
        adj_tiles.reshape(SLOTS, B, B), tile_rows.reshape(SLOTS),
        tile_cols.reshape(SLOTS), tile_count.reshape(1),
    )


def solution(mesh):
    nodes = P(("row", "col"), None)
    return jax.shard_map(
        body,
        mesh=mesh,
        in_specs=(
            nodes,
            P(),
            nodes,
            P("row", "col", None, None, None),
            P("row", "col", None),
            P("row", "col", None),
            P("row", "col"),
        ),
        out_specs=(nodes, nodes),
        check_vma=False,
    )
```

time: 676 us -> 111 us (0.16)
  waiting for transfers between devices: 642 us -> 0 us
  Pallas kernels: 0 us -> 104 us
  between operations: 14.6 us -> 1.31 us
    psum x2 -> x0, waiting for transfers between devices: 442 us -> none  [the longest x1 315 us: body(): summed_back = lax.psum(partial_back, 'row')]
    all_gather x2 -> x0, waiting for transfers between devices: 200 us -> none  [the longest x1 156 us: body(): column_block = lax.all_gather(features, 'row', axis=0, tiled=True)]
    pallas_call x0 -> x1, Pallas kernels: none -> 104 us  [body(): pl.pallas_call(kernel, out_shape=[jax.ShapeDtypeStruct((B, B), F32)] * 2,...]
  transfers between devices with their start and end apart: 4 -> 0, of which waited for: 4 -> 0; matrix products, arithmetic and copies ran while one was open for 0% -> 0% of each run, Pallas kernels for 0% -> 0%
where the time goes in v1:
time: 111 us
  Pallas kernels  104 us (94%)
  local copies, waits for them, and re-layouts  5.47 us (5%)
  between operations  1.31 us (1%)
    pallas_call x1, Pallas kernels, body(): pl.pallas_call(kernel, out_shape=[jax.ShapeDtypeStruct((B, B), F32)] * 2,...  104 us
    unnamed x14, local copies, waits for them, and re-layouts  5.47 us

profile of v1, /device:TPU:2, one launch (start us, length us, event | category | flops | bytes accessed | tf_op | source)
XLA Modules:
  0.0 110.7 jit_solution(11392638706545003495)
XLA Ops:
  1.3 0.0 copy-start.4
  1.3 0.0 copy-start.5
  1.3 0.6 copy-done.4
  1.9 0.0 copy-done.5
  2.0 0.0 copy-start
  2.0 1.0 copy-done
  3.0 0.0 copy-start.1
  3.0 0.8 copy-done.1
  3.8 0.0 copy-start.2
  3.8 0.8 copy-done.2
  4.7 0.0 copy-start.3
  4.7 0.8 copy-done.3
  5.5 103.9 %graph_layer.1 = (f32[128,128]{1,0:T(8,128)S(1)}, f32[128,128]{1,0:T(8,128)S(1)}) custom-call(f32[128,128]{1,0:T(8,128)S(1)} %copy-done.1, f32[128,128]{1,0:T(8,128)S(1)} %copy-done.2, f32[128,128]{1,0:T(8,128)S(1)} %copy-done.3, bf16[16,128,128]{2,1,0:T(8,128)(2,1)S(1)} %bitcast.5, s32[16]{0:T(128)S(1)} %bitcast.6, s32[16]{0:T(128)S(1)} %bitcast.7, ...), custom_call_target="tpu_custom_call" | custom-call | tf_op jit(solution)/shard_map/graph_layer/pallas_call | solution.py:213
  109.4 0.6 copy.12
  110.0 0.6 copy.13
Async XLA Ops:
  1.3 0.7 copy-start.4
  1.3 0.7 copy-start.5
  2.0 1.0 copy-start
  3.0 0.8 copy-start.1
  3.8 0.8 copy-start.2
  4.7 0.8 copy-start.3

commit v2 on v1

v2 whole, which is shorter than its diff:
```python
import functools

import jax
import jax.numpy as jnp
from jax import lax
from jax.experimental import pallas as pl
from jax.experimental.pallas import tpu as pltpu
from jax.sharding import PartitionSpec as P

F32 = jnp.float32
BF16 = jnp.bfloat16
MESH = pl.DeviceIdType.MESH
B = 128
SLOTS = 16
NZ = 16
SIGN = (1, -1)
CUT = 32
CHIPS = ((1, 2), (0, 2), (1, 1), (1, 3), (0, 1), (0, 3), (1, 0), (0, 0))


def span(t, d, dist):
    n = CUT if t else B
    return (0, n) if dist < 8 else (d * (n // 2), n // 2)


def split(value, parts):
    out = []
    for _ in range(parts - 1):
        head = value.astype(BF16)
        out.append(head)
        value = value - head.astype(F32)
    out.append(value.astype(BF16))
    return out


def two_sum(a, b):
    total = a + b
    shown = total - a
    return total, (a - (total - shown)) + (b - shown)


def tile_product(tile, value, parts, transposed):
    dims = (((0,), (0,)), ((), ())) if transposed else (((1,), (0,)), ((), ()))
    total = None
    for part in reversed(split(value, parts)):
        term = lax.dot_general(tile, part, dims, preferred_element_type=F32)
        total = term if total is None else total + term
    return total


def kernel(
    feat, weight_hbm, grad_hbm, tiles_hbm, rows_hbm, cols_hbm, count_hbm,
    act, grad_in,
    rows, cols, count, own_feat, weight, grad_out, fbuf, tiles, acc, stage, sib, outb, rin, rowbuf, snd, rsin, ysend, yrecv, total1, hx,
    prev_r, prev_c, last_r, last_c,
    in_sem, px_s, px_r, ya_s, ya_r, ag_s, ag_r, sb_s, sb_r, rc_s, rc_r, cg_s, cg_r, cs_s, cs_r, yr_s, yr_r, rs_s, rs_r, hx_s, hx_r,
):
    me_row = lax.axis_index("row")
    me_col = lax.axis_index("col")
    z, h = me_row // 2, lax.rem(me_row, 2)
    core = lax.rem(me_col, 2)
    chip = me_col // 2
    y, x = chip // 4, lax.rem(chip, 4)

    def row_id(zz, q):
        return lax.rem(zz + 2 * NZ, NZ) * 2 + (h if q == 0 else 1 - h)

    def chip_to(k):
        dy, dx = CHIPS[k]
        return (lax.rem(y + dy, 2)) * 4 + lax.rem(x + dx, 4)

    def chip_from(k):
        dy, dx = CHIPS[k]
        return (lax.rem(y + dy, 2)) * 4 + lax.rem(x + 4 - dx, 4)

    sends = []

    def send(src, dst, s_sem, r_sem, dev):
        copy = pltpu.make_async_remote_copy(
            src_ref=src, dst_ref=dst, send_sem=s_sem, recv_sem=r_sem,
            device_id=dev, device_id_type=MESH,
        )
        copy.start()
        sends.append(copy)
        return copy

    def z_dev(delta):
        return (row_id(z + delta, 0), me_col)

    partner = (row_id(z, 1), me_col)
    sibling = (me_row, chip * 2 + 1 - core)
    peers = [(me_row, chip_to(k) * 2 + core) for k in range(7)]

    own_copy = pltpu.make_async_copy(feat, own_feat, in_sem.at[0])
    tile_copy = pltpu.make_async_copy(tiles_hbm, tiles, in_sem.at[1])
    weight_copy = pltpu.make_async_copy(weight_hbm, weight, in_sem.at[2])
    grad_copy = pltpu.make_async_copy(grad_hbm, grad_out, in_sem.at[3])
    index_copies = [
        pltpu.make_async_copy(src, dst, in_sem.at[4 + k])
        for k, (src, dst) in enumerate(((rows_hbm, rows), (cols_hbm, cols), (count_hbm, count)))
    ]
    for copy in index_copies + [own_copy, tile_copy, weight_copy, grad_copy]:
        copy.start()

    barrier = pltpu.get_barrier_semaphore()
    everyone = [z_dev(step) for step in (-2, -1, 1, 2)] + [partner, sibling] + peers
    for dev in everyone:
        pl.semaphore_signal(barrier, inc=1, device_id=dev, device_id_type=MESH)
    own_copy.wait()
    weight_copy.wait()
    fbuf[me_row] = jnp.dot(
        own_feat[...], weight[...], precision=lax.Precision.HIGHEST, preferred_element_type=F32
    )
    pl.semaphore_wait(barrier, len(everyone))

    def held(dist, d, q):
        return row_id(z - SIGN[d] * dist, q)

    def along(t, d, dist, step):
        lo, rows_n = span(t, d, dist)
        block = fbuf.at[held(dist - step, d, t), pl.ds(lo, rows_n)]
        src = block
        ag[t, d, dist] = send(
            src, block, ag_s.at[t, d, dist - 1], ag_r.at[t, d, dist - 1], z_dev(SIGN[d] * step)
        )

    def onward(t, dist):
        for d in range(2):
            if dist > 0:
                ag[t, d, dist].wait_recv()
            along(t, d, dist + 2, 2)
        for d in range(2):
            along(t, d, dist + 1, 1)

    def across(d, dist):
        lo, rows_n = span(0, d, dist)
        lo, rows_n = max(lo, CUT), lo + rows_n - max(lo, CUT)
        block = fbuf.at[held(dist, d, 0), pl.ds(lo, rows_n)]
        src = block
        ya.append(send(src, block, ya_s.at[d, dist], ya_r.at[d, dist], partner))

    ag, ya = {}, []
    first = fbuf.at[me_row, pl.ds(0, CUT)]
    px = send(first, first, px_s, px_r, partner)
    onward(0, 0)
    across(0, 0)

    for copy in index_copies:
        copy.wait()
    live = count[0]
    key_r = [jnp.where(t < live, rows[t], -1 - t) for t in range(SLOTS)]
    key_c = [jnp.where(t < live, cols[t], -1 - t) for t in range(SLOTS)]
    for t in range(SLOTS):
        pr, pc = jnp.int32(SLOTS), jnp.int32(SLOTS)
        for u in range(t):
            pr = jnp.where(key_r[u] == key_r[t], u, pr)
            pc = jnp.where(key_c[u] == key_c[t], u, pc)
        prev_r[t] = pr
        prev_c[t] = pc
    for r in range(16):
        last = jnp.int32(SLOTS)
        for t in range(SLOTS):
            last = jnp.where(key_r[t] == r, t, last)
        last_r[r] = last
    for r in range(32):
        last = jnp.int32(SLOTS)
        for t in range(SLOTS):
            last = jnp.where(key_c[t] == r, t, last)
        last_c[r] = last
    acc[SLOTS] = jnp.zeros((B, B), F32)

    px.wait_recv()
    onward(1, 0)
    for dist in (2, 4, 6):
        onward(0, dist)
        for near in (dist - 1, dist):
            for d in range(2):
                if near < dist:
                    ag[0, d, near].wait_recv()
                across(d, near)
        onward(1, dist)
    for dist in (7, 8):
        for d in range(2):
            ag[0, d, dist].wait_recv()
            across(d, dist)
    for d in range(2):
        for dist in (1, 3, 5, 7, 8):
            ag[1, d, dist].wait_recv()
    for copy in ya:
        copy.wait_recv()

    tile_copy.wait()
    grad_copy.wait()
    for t in range(SLOTS):
        acc[t] = tile_product(tiles[t], fbuf[cols[t]], 3, False) + acc[prev_r[t]]

    sb, rc = [], []
    for k in range(8):
        stage[k] = acc[last_r[chip_to(k) * 2 + 1 - core]]
        sb.append(send(stage.at[k], sib.at[k], sb_s.at[k], sb_r.at[k], sibling))
    for k in range(8):
        mine = acc[last_r[chip_to(k) * 2 + core]]
        sb[k].wait_recv()
        outb[k] = mine + sib[k]
        if k < 7:
            rc.append(send(outb.at[k], rin.at[k], rc_s.at[k], rc_r.at[k], peers[k]))
    pre, rest = outb[7], jnp.zeros((B, B), F32)
    for k in reversed(range(7)):
        rc[k].wait_recv()
        pre, error = two_sum(pre, rin[k])
        rest = rest + error
    pre = pre + rest
    masked = jnp.where(pre > 0.0, grad_out[...], 0.0)
    rowbuf[me_col] = lax.dot_general(
        masked, weight[...], (((1,), (1,)), ((), ())),
        precision=lax.Precision.HIGHEST, preferred_element_type=F32,
    )

    cg, cs = [], []
    own = rowbuf.at[me_col]
    for k in range(7):
        cg.append(send(own, own, cg_s.at[k], cg_r.at[k], peers[k]))
    cs.append(send(own, own, cs_s.at[7], cs_r.at[7], sibling))
    act[...] = jnp.maximum(pre, 0.0)
    for k in reversed(range(7)):
        cg[k].wait_recv()
        block = rowbuf.at[chip_from(k) * 2 + core]
        cs.append(send(block, block, cs_s.at[k], cs_r.at[k], sibling))
    for copy in cs:
        copy.wait_recv()

    for t in range(SLOTS):
        acc[t] = tile_product(tiles[t], rowbuf[rows[t]], 2, True) + acc[prev_c[t]]

    order = [(0, 8)] + [(d, dist) for dist in range(7, 0, -1) for d in range(2)] + [(0, 0)]
    slot_of = {key: k for k, key in enumerate(order)}
    slot_of[1, 8] = 0
    yr = []
    for k, (d, dist) in enumerate(order):
        ysend[k] = acc[last_c[row_id(z + SIGN[d] * dist, 1)], pl.ds(CUT, B - CUT)]
        yr.append(send(ysend.at[k], yrecv.at[k], yr_s.at[k], yr_r.at[k], partner))

    rs, arrived = {}, set()

    def running(t, d, dist, lo, n):
        value = acc[last_c[row_id(z + SIGN[d] * dist, t)], pl.ds(lo, n)]
        if t == 0 and lo >= CUT:
            value = value + yrecv[slot_of[d, dist], pl.ds(lo - CUT, n)]
        for way in (0, 1) if dist == 0 else (d,):
            for back in (1, 2):
                key = t, way, dist + back
                if key in rs and dist % 2 == 0:
                    low, size = span(*key)
                    if low <= lo and lo + n <= low + size:
                        value = value + rsin[t, way, dist + back - 1, pl.ds(lo, n)]
        return value

    def pieces(t, d, dist):
        lo, n = span(t, d, dist)
        ends = {lo, lo + n}
        for edge in (CUT, span(t, 1, 8)[0]):
            if lo < edge < lo + n:
                ends.add(edge)
        ends = sorted(ends)
        return [(u, v - u) for u, v in zip(ends, ends[1:])]

    def await_parts(t, d, dist):
        if t == 0 and slot_of[d, dist] not in arrived:
            arrived.add(slot_of[d, dist])
            yr[slot_of[d, dist]].wait_recv()
        if dist % 2 == 0:
            for way in (0, 1) if dist == 0 else (d,):
                for back in (1, 2):
                    if dist + back <= 8:
                        rs[t, way, dist + back].wait_recv()

    for dist in (8, 7, 5, 6, 3, 4, 1, 2):
        for t in (1, 0):
            for d in range(2):
                await_parts(t, d, dist)
                for lo, n in pieces(t, d, dist):
                    snd[t, d, dist - 1, pl.ds(lo, n)] = running(t, d, dist, lo, n)
                lo, n = span(t, d, dist)
                at = t, d, dist - 1, pl.ds(lo, n)
                rs[t, d, dist] = send(
                    snd.at[at], rsin.at[at], rs_s.at[t, d, dist - 1], rs_r.at[t, d, dist - 1],
                    z_dev(SIGN[d] * (2 - dist % 2)),
                )
    await_parts(1, 0, 0)
    total1[...] = running(1, 0, 0, 0, CUT)
    last = send(total1, hx, hx_s, hx_r, partner)
    await_parts(0, 0, 0)
    grad_in[pl.ds(CUT, B - CUT)] = running(0, 0, 0, CUT, B - CUT)
    head = running(0, 0, 0, 0, CUT)
    last.wait_recv()
    grad_in[pl.ds(0, CUT)] = head + hx[...]

    for copy in sends:
        copy.wait_send()


def body(features, weight, grad_out, adj_tiles, tile_rows, tile_cols, tile_count):
    vmem = pl.BlockSpec(memory_space=pltpu.VMEM)
    dma = pltpu.SemaphoreType.DMA
    return pl.pallas_call(
        kernel,
        out_shape=[jax.ShapeDtypeStruct((B, B), F32)] * 2,
        in_specs=[pl.BlockSpec(memory_space=pl.ANY)] * 7,
        out_specs=[vmem, vmem],
        scratch_shapes=[
            pltpu.SMEM((SLOTS,), jnp.int32),
            pltpu.SMEM((SLOTS,), jnp.int32),
            pltpu.SMEM((1,), jnp.int32),
            pltpu.VMEM((B, B), F32),
            pltpu.VMEM((B, B), F32),
            pltpu.VMEM((B, B), F32),
            pltpu.VMEM((32, B, B), F32),
            pltpu.VMEM((SLOTS, B, B), BF16),
            pltpu.VMEM((SLOTS + 1, B, B), F32),
            pltpu.VMEM((8, B, B), F32),
            pltpu.VMEM((8, B, B), F32),
            pltpu.VMEM((8, B, B), F32),
            pltpu.VMEM((7, B, B), F32),
            pltpu.VMEM((16, B, B), F32),
            pltpu.VMEM((2, 2, 8, B, B), F32),
            pltpu.VMEM((2, 2, 8, B, B), F32),
            pltpu.VMEM((16, B - CUT, B), F32),
            pltpu.VMEM((16, B - CUT, B), F32),
            pltpu.VMEM((CUT, B), F32),
            pltpu.VMEM((CUT, B), F32),
            pltpu.SMEM((SLOTS,), jnp.int32),
            pltpu.SMEM((SLOTS,), jnp.int32),
            pltpu.SMEM((16,), jnp.int32),
            pltpu.SMEM((32,), jnp.int32),
            dma((7,)), dma(()), dma(()),
            dma((2, 9)), dma((2, 9)),
            dma((2, 2, 8)), dma((2, 2, 8)),
            dma((8,)), dma((8,)),
            dma((7,)), dma((7,)),
            dma((7,)), dma((7,)),
            dma((8,)), dma((8,)),
            dma((16,)), dma((16,)),
            dma((2, 2, 8)), dma((2, 2, 8)),
            dma(()), dma(()),
        ],
        compiler_params=pltpu.CompilerParams(
            collective_id=0, has_side_effects=True, vmem_limit_bytes=62 * 1024 * 1024
        ),
        name="graph_layer",
    )(
        features, weight, grad_out,
        adj_tiles.reshape(SLOTS, B, B), tile_rows.reshape(SLOTS),
        tile_cols.reshape(SLOTS), tile_count.reshape(1),
    )


def solution(mesh):
    nodes = P(("row", "col"), None)
    return jax.shard_map(
        body,
        mesh=mesh,
        in_specs=(
            nodes,
            P(),
            nodes,
            P("row", "col", None, None, None),
            P("row", "col", None),
            P("row", "col", None),
            P("row", "col"),
        ),
        out_specs=(nodes, nodes),
        check_vma=False,
    )
```

time: 111 us -> 95.8 us (0.86)
  the two profiles are of different devices: /device:TPU:2 before, /device:TPU:8 now
where the time goes in v2:
time: 95.8 us; the launch traced here: 95.6 us
  Pallas kernels  92.2 us (96%)
  local copies, waits for them, and re-layouts  2.14 us (2%)
  between operations  1.3 us (1%)
    pallas_call x1, Pallas kernels, body(): pl.pallas_call(kernel, out_shape=[jax.ShapeDtypeStruct((B, B), F32)] * 2,...  92.2 us
    unnamed x4, local copies, waits for them, and re-layouts  2.14 us

profile of v2, /device:TPU:8, one launch (start us, length us, event | category | flops | bytes accessed | tf_op | source)
XLA Modules:
  0.0 95.6 jit_solution(17990111781477123234)
XLA Ops:
  1.3 92.2 %graph_layer.1 = (f32[128,128]{1,0:T(8,128)}, f32[128,128]{1,0:T(8,128)}) custom-call(f32[128,128]{1,0:T(8,128)} %feat.1, f32[128,128]{1,0:T(8,128)} %weight_hbm.1, f32[128,128]{1,0:T(8,128)} %grad_hbm.1, bf16[16,128,128]{2,1,0:T(8,128)(2,1)} %bitcast.5, s32[16]{0:T(128)} %bitcast.6, s32[16]{0:T(128)} %bitcast.7, s32[1]{0:T(128)} %bitcast.4.count_hbm), custom_call_target="tpu_custom_call" | custom-call | tf_op jit(solution)/shard_map/graph_layer/pallas_call | solution.py:305
  93.5 0.0 copy-start
  93.5 1.5 %copy.12 = f32[128,128]{1,0:T(8,128)} copy(f32[128,128]{1,0:T(8,128)} %get-tuple-element.4) | data formatting | bytes 131072
  95.0 0.0 copy-done
  95.0 0.6 copy.13
Async XLA Ops:
  93.5 1.5 %copy-start = (f32[128,128]{1,0:T(8,128)S(1)}, f32[128,128]{1,0:T(8,128)}, u32[]{:S(2)}) copy-start(f32[128,128]{1,0:T(8,128)} %get-tuple-element.5) | copy-start | bytes 196612
